TPU v7x, 32 devices: a whole 2x2x4 slice. The times are simulated.
32 devices in a mesh: cell: 8 (over z, y), stn: 4 (over x, core).
Axes of the slice: x: 2, y: 2, z: 4, core: 2. Of those that a mesh axis runs over, the one named last changes fastest.
Arguments:
- cell_points: float32 [3, 8192], P(None, 'cell'), may hold values from 0 to 1
- magnetization: float32 [3, 8192], P(None, 'cell'), may hold values from -6 to 6
- cell_level: int32 [8192], P('cell'), may hold values from 0 to 2
- suscept: float32 [8192], P('cell'), may hold values from 0.2 to 2
- inducing: float32 [3], replicated, may hold values from -4 to 4
- stations: float32 [3, 4096], P(None, 'stn'), may hold values from 0 to 2, as said below
Outputs:
- updated: float32 [3, 8192], P(None, ('cell', 'stn'))
- predictions: float32 [4096], P(('stn', 'cell'))
Inputs may be any that keep to these rules, and one draw needn't show every extreme that they name: `stations`: the first two coordinates lie in the unit square; the third is 1 plus 0.5 to 2 times 8192 ** (-1/3).
All inputs are finite; a program needn't handle non-finite values.
Results may differ from a plain program's by a relative error of at most 0.0003.
Values sent between devices are 32-bit elements; how exact they have to be, the bound alone decides.
A program may use at most 64 MiB of HBM per device.

v0:
```python
import math
import jax
import jax.numpy as jnp
from jax import lax
from jax.sharding import PartitionSpec as P

INV_FOUR_PI = 0.25 / math.pi


def block_width(targets, sources):
    ceiling = max(256, (1 << 20) // targets)
    ceiling = 1 << ceiling.bit_length() - 1
    return math.gcd(sources, ceiling)


def pair_field(points, source_piece):
    delta_x = points[0][:, None] - source_piece[0][None, :]
    delta_y = points[1][:, None] - source_piece[1][None, :]
    delta_z = points[2][:, None] - source_piece[2][None, :]
    soften = source_piece[6][None, :]
    radius_sq = delta_x * delta_x + delta_y * delta_y + delta_z * delta_z + soften * soften
    inverse = lax.rsqrt(radius_sq)
    inverse_sq = inverse * inverse
    weight = INV_FOUR_PI * soften * soften * soften * inverse_sq * inverse
    projection = (
        3.0
        * (
            delta_x * source_piece[3][None, :]
            + delta_y * source_piece[4][None, :]
            + delta_z * source_piece[5][None, :]
        )
        * inverse_sq
    )
    field_x = jnp.sum(weight * (projection * delta_x - source_piece[3][None, :]), axis=1)
    field_y = jnp.sum(weight * (projection * delta_y - source_piece[4][None, :]), axis=1)
    field_z = jnp.sum(weight * (projection * delta_z - source_piece[5][None, :]), axis=1)
    return jnp.stack([field_x, field_y, field_z], 0)


def source_field(points, sources):
    number = sources.shape[1]
    blockw = block_width(points.shape[1], number)
    groups = sources.reshape(7, number // blockw, blockw).transpose(1, 0, 2)

    def advance(summed, source_piece):
        return (summed + pair_field(points, source_piece), None)

    result, unused = lax.scan(advance, jnp.zeros((3, points.shape[1]), jnp.float32), groups)
    return result


def shards(cell_points, magnetization, cell_level, suscept, inducing, stations):
    cycle_size = lax.axis_size("cell")
    section = lax.axis_size("stn")
    block_cells = cell_points.shape[1]
    spacing = float(block_cells * cycle_size * section // section) ** (-1.0 / 3.0)
    size_h = spacing * jnp.power(0.5, cell_level.astype(jnp.float32))
    packed = jnp.concatenate([cell_points, magnetization, size_h[None, :]], 0)
    owned = block_cells // section
    offset = lax.axis_index("stn") * owned
    targets = lax.dynamic_slice_in_dim(cell_points, offset, owned, 1)
    demag = source_field(targets, lax.all_gather(packed, "cell", axis=1, tiled=True))
    own_suscept = lax.dynamic_slice_in_dim(suscept, offset, owned, 0)
    updated = own_suscept[None, :] * (inducing[:, None] + demag)
    block_mag = lax.all_gather(updated, "stn", axis=1, tiled=True)
    moved = jnp.concatenate([cell_points, block_mag, size_h[None, :]], 0)
    field = source_field(stations, moved)
    predictions = lax.psum_scatter(
        jnp.sum(inducing[:, None] * field, axis=0), "cell", scatter_dimension=0, tiled=True
    )
    return (updated, predictions)


def solution(mesh):
    placed = (P(None, "cell"), P(None, "cell"), P("cell"), P("cell"), P(), P(None, "stn"))
    return jax.shard_map(
        shards,
        mesh=mesh,
        in_specs=placed,
        out_specs=(P(None, ("cell", "stn")), P(("stn", "cell"))),
        check_vma=False,
    )
```

profile of v0, /device:TPU:0, one launch (start us, length us, event | category | flops | bytes accessed | tf_op | source)
XLA Modules:
  0.0 82.9 jit_solution(14544340827631167878)
XLA Ops:
  0.6 0.7 constant_dynamic-slice_fusion.7
  1.3 0.7 multiply_multiply_fusion.3
  2.0 0.8 pad_maximum_fusion
  2.8 32.5 %all_gather.6 = f32[7,8192]{1,0:T(8,128)S(1)} all-gather(f32[7,1024]{1,0:T(8,128)S(1)} %pad_maximum_fusion), channel_id=1, replica_groups=mesh['cell'=8,'stn'=4] {'cell'}, dimensions={1}, use_global_device_ids=true | all-gather | bytes 258048 | tf_op jit(solution)/shard_map/all_gather | solution.py:62
  35.3 0.0 copy-start.3
  35.3 0.0 copy-start.2
  35.3 0.0 copy-start
  35.3 11.8 %while.3 = (s32[]{:T(128)}, f32[3,256]{1,0:T(4,128)S(1)}, f32[2,7,4096]{2,1,0:T(8,128)S(1)}, f32[3,256]{1,0:T(4,128)S(1)}, s32[]{:T(128)}, /*index=5*/s32[]{:T(128)}, s32[]{}, s32[]{}, s32[]{}, s32[]{}, /*index=10*/s32[]{}, s32[]{}) while((s32[]{:T(128)}, f32[3,256]{1,0:T(4,128)S(1)}, f32[2,7,4096]{2,1,0:T(8,128)S(1)}, ...), condition=%wide.region_4.5_spmd.clone, body=%wide.region_0.4_spmd.clone.sunk | while | flops 32524552 | bytes 431331 | solution.py:48
  35.3 0.1 constant_dynamic-slice_fusion.9
  35.5 5.7 %fusion.44 = (f32[256]{0:T(256)S(1)}, f32[256]{0:T(256)S(1)}, f32[256]{0:T(256)S(1)}) fusion(f32[4096]{0:T(1024)S(1)} %bitcast.60, f32[4096]{0:T(1024)S(1)} %bitcast.62, f32[256]{0:T(256)S(1)} %bitcast.69, f32[4096]{0:T(1024)S(1)} %get-tuple-element.134, f32[4096]{0:T(1024)S(1)} %bitcast.63, f32[4096]{0:T(1024)S(1)} %bitcast.61, f32[256]{0:T(256)S(1)} %bitcast.68, ...), kind=kLoop, calls=%fused_computation.19.clone.1 | loop fusion | flops 32505088 | bytes 137216 | tf_op jit(solution)/shard_map/while/body/eval_jaxpr/reduce_sum | solution.py:34
  41.2 0.1 constant_dynamic-slice_fusion.9
  41.4 5.7 %fusion.44 = (f32[256]{0:T(256)S(1)}, f32[256]{0:T(256)S(1)}, f32[256]{0:T(256)S(1)}) fusion(f32[4096]{0:T(1024)S(1)} %bitcast.60, f32[4096]{0:T(1024)S(1)} %bitcast.62, f32[256]{0:T(256)S(1)} %bitcast.69, f32[4096]{0:T(1024)S(1)} %get-tuple-element.134, f32[4096]{0:T(1024)S(1)} %bitcast.63, f32[4096]{0:T(1024)S(1)} %bitcast.61, f32[256]{0:T(256)S(1)} %bitcast.68, ...), kind=kLoop, calls=%fused_computation.19.clone.1 | loop fusion | flops 32505088 | bytes 137216 | tf_op jit(solution)/shard_map/while/body/eval_jaxpr/reduce_sum | solution.py:34
  47.2 0.8 dynamic_slice.13
  47.9 0.0 copy-done.3
  47.9 0.1 add_multiply_fusion
  48.0 0.0 copy-start.1
  48.0 5.2 %all_gather.7 = f32[3,1024]{1,0:T(4,128)S(1)} all-gather(f32[3,256]{1,0:T(4,128)S(1)} %add_multiply_fusion), channel_id=1, replica_groups=mesh['cell'=8,'stn'=4] {'stn'}, dimensions={1}, use_global_device_ids=true | all-gather | bytes 15360 | tf_op jit(solution)/shard_map/all_gather | solution.py:65
  53.2 0.0 copy-done.2
  53.2 0.0 copy-done
  53.2 0.0 copy-start.4
  53.3 6.2 %fusion.27 = (f32[1024]{0:T(1024)S(1)}, f32[1024]{0:T(1024)S(1)}, f32[1024]{0:T(1024)S(1)}) fusion(f32[1024]{0:T(1024)S(1)} %bitcast.73, f32[1024]{0:T(1024)S(1)} %bitcast.78, f32[1024]{0:T(1024)S(1)} %bitcast.75, f32[1024]{0:T(1024)S(1)} %get-tuple-element.88, f32[1024]{0:T(1024)S(1)} %bitcast.72, f32[1024]{0:T(1024)S(1)} %bitcast.79, ...), kind=kLoop, calls=%fused_computation.55 | loop fusion | flops 32502784 | bytes 57344 | tf_op jit(solution)/shard_map/while/body/eval_jaxpr/reduce_sum | solution.py:34
  59.5 0.0 copy-done.1
  59.5 0.1 fusion.34
  59.6 21.4 %all-reduce = f32[1024]{0:T(1024)S(1)} all-reduce(f32[1024]{0:T(1024)S(1)} %fusion.34), channel_id=2, replica_groups=mesh['cell'=8,'stn'=4] {'cell'}, use_global_device_ids=true, to_apply=%region_9.10.clone | all-reduce | flops 1024 | bytes 8192
  81.0 0.0 copy-done.4
  81.0 0.6 dynamic-slice.1
  82.3 0.6 dynamic-slice.2
  (10 shorter events, 0.1 us)
Async XLA Ops:
  35.3 12.6 %copy-start.3 = (f32[3]{0:T(128)S(1)}, f32[3]{0:T(128)}, u32[]{:S(2)}) copy-start(f32[3]{0:T(128)} %param.12) | copy-start | bytes 40
  35.3 17.9 %copy-start.2 = (f32[3,1024]{1,0:T(4,128)S(1)}, f32[3,1024]{1,0:T(4,128)}, u32[]{:S(2)}) copy-start(f32[3,1024]{1,0:T(4,128)} %param.13) | copy-start | bytes 36868
  35.3 17.9 %copy-start = (f32[3,1024]{1,0:T(4,128)S(1)}, f32[3,1024]{1,0:T(4,128)}, u32[]{:S(2)}) copy-start(f32[3,1024]{1,0:T(4,128)} %param.8) | copy-start | bytes 36868
  48.0 11.5 %copy-start.1 = (f32[3,256]{1,0:T(4,128)}, f32[3,256]{1,0:T(4,128)S(1)}, u32[]{:S(2)}) copy-start(f32[3,256]{1,0:T(4,128)S(1)} %add_multiply_fusion) | copy-start | bytes 9220
  53.2 27.8 %copy-start.4 = (u32[32]{0:T(128)S(1)}, u32[32]{0:T(128)}, u32[]{:S(2)}) copy-start(u32[32]{0:T(128)} %constant.48) | copy-start | bytes 388
where the time goes:
time: 83.3 us; the launch traced here: 82.9 us
  blocking collectives  59.1 us (71%)
  other arithmetic  19.4 us (23%)
  local copies, waits for them, and re-layouts  2.93 us (4%)
  between operations  1.37 us (2%)
    all_gather x1, blocking collectives, shards(): lax.all_gather(packed, 'cell', axis=1, tiled=True)  32.5 us
    unnamed x1, blocking collectives  21.4 us
    reduce_sum x3, other arithmetic, pair_field(): jnp.sum(weight * (projection * delta_x - source_piece[3][None, :]), axis=1)  17.7 us
    all_gather x1, blocking collectives, shards(): block_mag = lax.all_gather(updated, 'stn', axis=1, tiled=True)  5.17 us

commit v1 on v0

--- a/solution.py
+++ b/solution.py
@@ -1,3 +1,4 @@
+import functools
 import math
 import jax
 import jax.numpy as jnp
@@ -5,6 +6,24 @@
 from jax.sharding import PartitionSpec as P
 
 INV_FOUR_PI = 0.25 / math.pi
+
+
+def run_goods(field_in, device_axis):
+    u1, s_next = (jax.lax.axis_size(device_axis), jax.lax.axis_index(device_axis))
+    reached, lower = (field_in, 1)
+    while lower < u1:
+        panels = []
+        for jj in range(u1):
+            panels.append((jj, jj ^ lower))
+        inter = jax.lax.ppermute(reached, axis_name=device_axis, perm=panels)
+        tile_out = jnp.concatenate([reached, inter], axis=1)
+        carry_out = jnp.concatenate([inter, reached], axis=1)
+        reached = jnp.where(s_next & lower == 0, tile_out, carry_out)
+        lower = 2 * lower
+    return reached
+
+
+_rest_counts = functools.partial(run_goods, device_axis="cell")
 
 
 def block_width(targets, sources):
@@ -59,7 +78,7 @@
     owned = block_cells // section
     offset = lax.axis_index("stn") * owned
     targets = lax.dynamic_slice_in_dim(cell_points, offset, owned, 1)
-    demag = source_field(targets, lax.all_gather(packed, "cell", axis=1, tiled=True))
+    demag = source_field(targets, _rest_counts(packed))
     own_suscept = lax.dynamic_slice_in_dim(suscept, offset, owned, 0)
     updated = own_suscept[None, :] * (inducing[:, None] + demag)
     block_mag = lax.all_gather(updated, "stn", axis=1, tiled=True)

time: 83.3 us -> 67.8 us (0.81)
  blocking collectives: 59.1 us -> 25.7 us
  starting transfers between devices: 0 us -> 7.33 us
  waiting for transfers between devices: 0 us -> 6.91 us
  local copies, waits for them, and re-layouts: 2.93 us -> 5.23 us
    all_gather x1 -> x0, blocking collectives: 32.5 us -> none  [shards(): lax.all_gather(packed, 'cell', axis=1, tiled=True)]
    ppermute x0 -> x3, starting transfers between devices: none -> 7.33 us  [run_goods(): inter = jax.lax.ppermute(reached, axis_name=device_axis, perm=panels)]
    ppermute x0 -> x3, waiting for transfers between devices: none -> 6.91 us  [run_goods(): inter = jax.lax.ppermute(reached, axis_name=device_axis, perm=panels)]
    slice x6, local copies, waits for them, and re-layouts: 0.27 us -> 1.93 us  [pair_field(): delta_y = points[1][:, None] - source_piece[1][None, :]]
    unnamed x1, blocking collectives: 21.4 us -> 20.6 us
    select_n x0 -> x3, other arithmetic: none -> 0.86 us  [run_goods(): reached = jnp.where(s_next & lower == 0, tile_out, carry_out)]
    unnamed x12 -> x6, local copies, waits for them, and re-layouts: 1.19 us -> 1.83 us
  transfers between devices with their start and end apart: 0 -> 3, of which waited for: 0 -> 2; matrix products, arithmetic and copies ran while one was open for 0% -> 7% of each run, Pallas kernels for 0% -> 0%
where the time goes in v1:
time: 67.8 us; the launch traced here: 66.9 us
  blocking collectives  25.7 us (38%)
  other arithmetic  20.2 us (30%)
  starting transfers between devices  7.33 us (11%)
  waiting for transfers between devices  6.91 us (10%)
  local copies, waits for them, and re-layouts  5.23 us (8%)
  between operations  1.39 us (2%)
    unnamed x1, blocking collectives  20.6 us
    reduce_sum x3, other arithmetic, pair_field(): jnp.sum(weight * (projection * delta_x - source_piece[3][None, :]), axis=1)  17.7 us
    ppermute x3, starting transfers between devices, run_goods(): inter = jax.lax.ppermute(reached, axis_name=device_axis, perm=panels)  7.33 us
    ppermute x3, waiting for transfers between devices, run_goods(): inter = jax.lax.ppermute(reached, axis_name=device_axis, perm=panels)  6.91 us
    all_gather x1, blocking collectives, shards(): block_mag = lax.all_gather(updated, 'stn', axis=1, tiled=True)  5.17 us
    slice x6, local copies, waits for them, and re-layouts, pair_field(): delta_y = points[1][:, None] - source_piece[1][None, :]  1.93 us
    unnamed x6, local copies, waits for them, and re-layouts  1.83 us
  transfers between devices with their start and end apart: 3, of which 2 were waited for; matrix products, arithmetic and copies ran while one was open for 7% of the time, Pallas kernels for 0%

profile of v1, /device:TPU:0, one launch (start us, length us, event | category | flops | bytes accessed | tf_op | source)
XLA Modules:
  0.0 66.9 jit_solution(12091973498748408185)
XLA Ops:
  0.6 0.7 %multiply_multiply_fusion.3 = (f32[1024]{0:T(1024)S(1)}, f32[1024]{0:T(1024)S(1)}, f32[1024]{0:T(1024)S(1)}) fusion(s32[1024]{0:T(1024)} %param.10), kind=kLoop, calls=%fused_computation.71 | loop fusion | flops 6144 | bytes 16384 | tf_op jit(solution)/shard_map/while/body/eval_jaxpr/mul | solution.py:43
  1.3 0.8 %pad_maximum_fusion = f32[7,1024]{1,0:T(8,128)S(1)} fusion(f32[1,1024]{1,0:T(1,128)S(1)} %bitcast.68, f32[3,1024]{1,0:T(4,128)} %param.9, f32[3,1024]{1,0:T(4,128)} %param.8), kind=kLoop, calls=%fused_computation.68 | loop fusion | flops 14336 | bytes 57344 | tf_op jit(solution)/shard_map/concatenate | solution.py:77
  2.1 3.0 %collective-permute-start = (f32[7,1024]{1,0:T(8,128)S(1)}, f32[7,1024]{1,0:T(8,128)S(1)}, u32[]{:S(2)}, u32[]{:S(2)}) collective-permute-start(f32[7,1024]{1,0:T(8,128)S(1)} %pad_maximum_fusion), channel_id=1, source_target_pairs={{0,4},{4,0},{8,12},{12,8},{16,20},{20,16},{24,28},{28,24},{1,5},{5... | collective-permute-start | bytes 86024 | tf_op jit(solution)/shard_map/ppermute | solution.py:18
  5.1 0.8 %fusion.40 = (f32[1,1024]{1,0:T(1,128)S(1)}, f32[1,1024]{1,0:T(1,128)S(1)}, f32[1,1024]{1,0:T(1,128)S(1)}) fusion(f32[3,1024]{1,0:T(4,128)} %param.8), kind=kLoop, calls=%fused_computation.79 | loop fusion | bytes 24576 | tf_op jit(solution)/shard_map/while/body/eval_jaxpr/slice | solution.py:37
  6.0 0.8 %fusion.39 = (f32[1,1024]{1,0:T(1,128)S(1)}, f32[1,1024]{1,0:T(1,128)S(1)}, f32[1,1024]{1,0:T(1,128)S(1)}) fusion(f32[3,1024]{1,0:T(4,128)} %param.13), kind=kLoop, calls=%fused_computation.78 | loop fusion | bytes 24576 | tf_op jit(solution)/shard_map/while/body/eval_jaxpr/slice | solution.py:37
  6.8 0.8 %dynamic_slice.13 = f32[256]{0:T(256)S(1)} dynamic-slice(f32[1024]{0:T(1024)} %param.11, s32[]{:T(128)S(6)} %select_n.44), dynamic_slice_sizes={256} | dynamic-slice | bytes 2052 | tf_op jit(solution)/shard_map/dynamic_slice | solution.py:82
  7.6 1.2 %dynamic-slice.1 = u32[1]{0:T(128)} dynamic-slice(u32[32]{0:T(128)} %constant.59, u32[]{:T(128)S(6)} %add.90), dynamic_slice_sizes={1} | dynamic-slice | bytes 12
  9.5 0.0 collective-permute-done
  9.5 0.8 %maximum_select_fusion.3 = f32[7,2048]{1,0:T(8,128)S(1)} fusion(f32[7,1024]{1,0:T(8,128)S(1)} %collective-permute-done, f32[1,1024]{1,0:T(1,128)S(1)} %bitcast.69, f32[3,1024]{1,0:T(4,128)} %param.9, f32[3,1024]{1,0:T(4,128)} %param.8, pred[]{:T(512)S(6)} %eq.11), kind=kLoop, calls=%fused_computation.67 | loop fusion | flops 100352 | bytes 114689 | tf_op jit(solution)/shard_map/jit(_where)/select_n | solution.py:21
  10.3 1.6 %collective-permute-start.1 = (f32[7,2048]{1,0:T(8,128)S(1)}, f32[7,2048]{1,0:T(8,128)S(1)}, u32[]{:S(2)}, u32[]{:S(2)}) collective-permute-start(f32[7,2048]{1,0:T(8,128)S(1)} %maximum_select_fusion.3), channel_id=1, source_target_pairs={{0,8},{4,12},{8,0},{12,4},{16,24},{20,28},{24,16},{28,20},{1,9},{5... | collective-permute-start | bytes 172040 | tf_op jit(solution)/shard_map/ppermute | solution.py:18
  12.0 0.7 %constant_dynamic-slice_fusion.7 = f32[3,256]{1,0:T(4,128)S(1)} fusion(f32[3,1024]{1,0:T(4,128)} %param.8, s32[]{:T(128)S(6)} %select_n.44), kind=kLoop, calls=%fused_computation.76 | loop fusion | bytes 6148 | tf_op jit(solution)/shard_map/dynamic_slice | solution.py:80
  12.7 2.0 %collective-permute-done.1 = f32[7,2048]{1,0:T(8,128)S(1)} collective-permute-done((f32[7,2048]{1,0:T(8,128)S(1)}, f32[7,2048]{1,0:T(8,128)S(1)}, u32[]{:S(2)}, u32[]{:S(2)}) %collective-permute-start.1) | collective-permute-done | bytes 57376 | tf_op jit(solution)/shard_map/ppermute | solution.py:18
  14.7 2.7 %collective-permute-start.2 = (f32[7,4096]{1,0:T(8,128)S(1)}, f32[7,4096]{1,0:T(8,128)S(1)}, u32[]{:S(2)}, u32[]{:S(2)}) collective-permute-start(f32[7,4096]{1,0:T(8,128)S(1)} %maximum_select_fusion.2), channel_id=1, source_target_pairs={{0,16},{4,20},{8,24},{12,28},{16,0},{20,4},{24,8},{28,12},{1,17},{... | collective-permute-start | bytes 344072 | tf_op jit(solution)/shard_map/ppermute | solution.py:18
  17.4 4.9 %collective-permute-done.2 = f32[7,4096]{1,0:T(8,128)S(1)} collective-permute-done((f32[7,4096]{1,0:T(8,128)S(1)}, f32[7,4096]{1,0:T(8,128)S(1)}, u32[]{:S(2)}, u32[]{:S(2)}) %collective-permute-start.2) | collective-permute-done | bytes 114720 | tf_op jit(solution)/shard_map/ppermute | solution.py:18
  22.3 0.0 copy-start.1
  22.3 11.8 %while.3 = (s32[]{:T(128)}, f32[3,256]{1,0:T(4,128)S(1)}, f32[2,7,4096]{2,1,0:T(8,128)S(1)}, f32[3,256]{1,0:T(4,128)S(1)}, s32[]{:T(128)}, /*index=5*/s32[]{:T(128)}, s32[]{}, s32[]{}, s32[]{}, s32[]{}, /*index=10*/s32[]{}, s32[]{}) while((s32[]{:T(128)}, f32[3,256]{1,0:T(4,128)S(1)}, f32[2,7,4096]{2,1,0:T(8,128)S(1)}, ...), condition=%wide.region_4.5_spmd.clone, body=%wide.region_0.4_spmd.clone.sunk | while | flops 32524552 | bytes 431331 | solution.py:67
  22.3 0.1 constant_dynamic-slice_fusion.9
  22.5 5.7 %fusion.45 = (f32[256]{0:T(256)S(1)}, f32[256]{0:T(256)S(1)}, f32[256]{0:T(256)S(1)}) fusion(f32[4096]{0:T(1024)S(1)} %bitcast.62, f32[4096]{0:T(1024)S(1)} %bitcast.64, f32[256]{0:T(256)S(1)} %bitcast.75, f32[4096]{0:T(1024)S(1)} %get-tuple-element.134, f32[4096]{0:T(1024)S(1)} %bitcast.65, f32[4096]{0:T(1024)S(1)} %bitcast.63, f32[256]{0:T(256)S(1)} %bitcast.74, ...), kind=kLoop, calls=%fused_computation.19.clone.1 | loop fusion | flops 32505088 | bytes 137216 | tf_op jit(solution)/shard_map/while/body/eval_jaxpr/reduce_sum | solution.py:53
  28.2 0.1 constant_dynamic-slice_fusion.9
  28.4 5.7 %fusion.45 = (f32[256]{0:T(256)S(1)}, f32[256]{0:T(256)S(1)}, f32[256]{0:T(256)S(1)}) fusion(f32[4096]{0:T(1024)S(1)} %bitcast.62, f32[4096]{0:T(1024)S(1)} %bitcast.64, f32[256]{0:T(256)S(1)} %bitcast.75, f32[4096]{0:T(1024)S(1)} %get-tuple-element.134, f32[4096]{0:T(1024)S(1)} %bitcast.65, f32[4096]{0:T(1024)S(1)} %bitcast.63, f32[256]{0:T(256)S(1)} %bitcast.74, ...), kind=kLoop, calls=%fused_computation.19.clone.1 | loop fusion | flops 32505088 | bytes 137216 | tf_op jit(solution)/shard_map/while/body/eval_jaxpr/reduce_sum | solution.py:53
  34.2 0.0 copy-done.1
  34.2 0.1 add_multiply_fusion
  34.2 0.0 copy-start
  34.2 5.2 %all_gather.3 = f32[3,1024]{1,0:T(4,128)S(1)} all-gather(f32[3,256]{1,0:T(4,128)S(1)} %add_multiply_fusion), channel_id=1, replica_groups=mesh['cell'=8,'stn'=4] {'stn'}, dimensions={1}, use_global_device_ids=true | all-gather | bytes 15360 | tf_op jit(solution)/shard_map/all_gather | solution.py:84
  39.4 6.2 %fusion.27 = (f32[1024]{0:T(1024)S(1)}, f32[1024]{0:T(1024)S(1)}, f32[1024]{0:T(1024)S(1)}) fusion(f32[1024]{0:T(1024)S(1)} %bitcast.84, f32[1024]{0:T(1024)S(1)} %bitcast.77, f32[1024]{0:T(1024)S(1)} %bitcast.80, f32[1024]{0:T(1024)S(1)} %get-tuple-element.88, f32[1024]{0:T(1024)S(1)} %bitcast.83, f32[1024]{0:T(1024)S(1)} %bitcast.78, ...), kind=kLoop, calls=%fused_computation.55 | loop fusion | flops 32502784 | bytes 57344 | tf_op jit(solution)/shard_map/while/body/eval_jaxpr/reduce_sum | solution.py:53
  45.7 0.0 copy-done
  45.7 0.1 fusion.35
  45.8 20.6 %all-reduce = f32[1024]{0:T(1024)S(1)} all-reduce(f32[1024]{0:T(1024)S(1)} %fusion.35), channel_id=2, replica_groups=mesh['cell'=8,'stn'=4] {'cell'}, use_global_device_ids=true, to_apply=%region_9.10.clone | all-reduce | flops 1024 | bytes 8192
  66.3 0.6 dynamic-slice.2
  (11 shorter events, 0.1 us)
Async XLA Ops:
  2.1 7.4 %collective-permute-start = (f32[7,1024]{1,0:T(8,128)S(1)}, f32[7,1024]{1,0:T(8,128)S(1)}, u32[]{:S(2)}, u32[]{:S(2)}) collective-permute-start(f32[7,1024]{1,0:T(8,128)S(1)} %pad_maximum_fusion), channel_id=1, source_target_pairs={{0,4},{4,0},{8,12},{12,8},{16,20},{20,16},{24,28},{28,24},{1,5},{5... | collective-permute-start | bytes 86024 | tf_op jit(solution)/shard_map/ppermute | solution.py:18
  10.3 4.3 %collective-permute-start.1 = (f32[7,2048]{1,0:T(8,128)S(1)}, f32[7,2048]{1,0:T(8,128)S(1)}, u32[]{:S(2)}, u32[]{:S(2)}) collective-permute-start(f32[7,2048]{1,0:T(8,128)S(1)} %maximum_select_fusion.3), channel_id=1, source_target_pairs={{0,8},{4,12},{8,0},{12,4},{16,24},{20,28},{24,16},{28,20},{1,9},{5... | collective-permute-start | bytes 172040 | tf_op jit(solution)/shard_map/ppermute | solution.py:18
  14.7 7.6 %collective-permute-start.2 = (f32[7,4096]{1,0:T(8,128)S(1)}, f32[7,4096]{1,0:T(8,128)S(1)}, u32[]{:S(2)}, u32[]{:S(2)}) collective-permute-start(f32[7,4096]{1,0:T(8,128)S(1)} %maximum_select_fusion.2), channel_id=1, source_target_pairs={{0,16},{4,20},{8,24},{12,28},{16,0},{20,4},{24,8},{28,12},{1,17},{... | collective-permute-start | bytes 344072 | tf_op jit(solution)/shard_map/ppermute | solution.py:18
  22.3 11.9 %copy-start.1 = (f32[3]{0:T(128)S(1)}, f32[3]{0:T(128)}, u32[]{:S(2)}) copy-start(f32[3]{0:T(128)} %param.12) | copy-start | bytes 40
  34.2 11.4 %copy-start = (f32[3,256]{1,0:T(4,128)}, f32[3,256]{1,0:T(4,128)S(1)}, u32[]{:S(2)}) copy-start(f32[3,256]{1,0:T(4,128)S(1)} %add_multiply_fusion) | copy-start | bytes 9220
